TPU v7x, 256 devices: a whole 4x4x8 slice. The times are simulated.
256 devices in a mesh: rows: 16 (over y, x), cls: 16 (over z, core).
Axes of the slice: x: 4, y: 4, z: 8, core: 2. Of those that a mesh axis runs over, the one named last changes fastest.
Arguments:
- soft_labels: bfloat16 [8192, 22016], P('rows', 'cls'), may hold values from 0 to 150, as said below
- features: bfloat16 [8192, 768], P('rows'), may hold values from -400 to 400
- neighbours: int32 [64, 5], replicated, may hold values from 0 to 63, as said below
- web_labels: int32 [8192], P('rows'), may hold values from 0 to 22015
Outputs:
- labels: bfloat16 [8192, 22016], P('rows', 'cls')
- prototypes: float32 [768, 22016], P('rows', 'cls')
Inputs may be any that keep to these rules, and one draw needn't show every extreme that they name: `neighbours`: block n holds samples n*128 to n*128 + 127, and index r of rows holds blocks r*4 to r*4 + 3. The 20 entries of the blocks of one index of rows, taken together, name the blocks of any one index of rows at most 2 times, and exactly 2 times for some index. A block may name itself or name a block more than once. `soft_labels`: Positive.
All inputs are finite; a program needn't handle non-finite values.
Results may differ from a plain program's by a relative error of at most 0.03.
Values may be sent and summed in bfloat16 or wider, within the bound.
A program may use at most 128 MiB of HBM per device.

v0:
```python
import jax
import jax.numpy as jnp
from jax import lax
from jax.sharding import PartitionSpec as P

C = 22016
FEATURE_WIDTH = 768
BLOCK_SAMPLES = 128


BOOST_FACTOR = 20.0
MIXING = 0.5
SOFTMAX_HEAT = 0.02
EPSILON_FEATURE = 1e-05
EPSILON_PROTO = 1e-06


def row_mass(values):
    return lax.psum(jnp.sum(values, axis=1), "cls")


def routing(neighbours, local_blocks, slots_cap):
    devices = lax.axis_size("rows")
    refs = local_blocks * neighbours.shape[1]
    table = neighbours.reshape(devices, refs)
    source = table // local_blocks
    within = table % local_blocks
    counter = jnp.arange(refs, dtype=jnp.int32)
    earlier = counter[None, :] < counter[:, None]
    same = source[:, :, None] == source[:, None, :]
    rank = jnp.sum(same & earlier[None, :, :], axis=2)
    device_here = lax.axis_index("rows")
    slot_ids = jnp.arange(slots_cap, dtype=jnp.int32)
    picked = (source[:, None, :] == device_here) & (rank[:, None, :] == slot_ids[None, :, None])
    filled = jnp.any(picked, axis=2).reshape(-1)
    chosen = jnp.sum(jnp.where(picked, within[:, None, :], 0), axis=2).reshape(-1)
    own_source = lax.dynamic_index_in_dim(source, device_here, 0, keepdims=False)
    own_rank = lax.dynamic_index_in_dim(rank, device_here, 0, keepdims=False)
    slot_of_ref = own_source * slots_cap + own_rank
    return (chosen, filled, slot_of_ref)


def pack_tiles(data, chosen, filled):
    tiles = jnp.take(data.reshape(-1, BLOCK_SAMPLES, data.shape[1]), chosen, axis=0)
    return jnp.where(filled[:, None, None], tiles, jnp.zeros_like(tiles))


def unpack_tiles(received, slot_of_ref, local_blocks):
    picked = jnp.take(received, slot_of_ref, axis=0)
    return picked.reshape(local_blocks, -1, received.shape[2])


def neighbour_labels(data, chosen, filled, slot_of_ref, local_blocks):
    received = lax.all_to_all(
        pack_tiles(data, chosen, filled), "rows", split_axis=0, concat_axis=0, tiled=True
    )
    return unpack_tiles(received, slot_of_ref, local_blocks)


def body(soft_labels, features, neighbours, web_labels):
    local_blocks = soft_labels.shape[0] // BLOCK_SAMPLES
    width = soft_labels.shape[1]
    neighbour_count = neighbours.shape[1]
    devices = lax.axis_size("rows")
    slots_cap = max(2, -(-(local_blocks * neighbour_count) // devices))
    device_here = lax.axis_index("rows")
    offset = lax.axis_index("cls") * width
    hits = web_labels[:, None] == offset + jnp.arange(width, dtype=jnp.int32)[None, :]
    boosted = soft_labels.astype(jnp.float32) * jnp.where(hits, 1.0 + BOOST_FACTOR, 1.0)
    prior = (C * boosted / row_mass(boosted)[:, None]).astype(jnp.bfloat16)
    feature_wide = features.astype(jnp.float32)
    fnorm = (
        feature_wide
        / jnp.sqrt(jnp.mean(feature_wide * feature_wide, axis=1, keepdims=True) + EPSILON_FEATURE)
    ).astype(jnp.bfloat16)
    chosen, filled, slot_of_ref = routing(neighbours, local_blocks, slots_cap)
    listed = lax.dynamic_slice_in_dim(neighbours, device_here * local_blocks, local_blocks, 0)
    feature_tiles, prior_tiles = (
        lax.all_to_all(
            pack_tiles(fnorm, chosen, filled), "rows", split_axis=0, concat_axis=0, tiled=True
        ),
        lax.all_to_all(
            pack_tiles(prior, chosen, filled), "rows", split_axis=0, concat_axis=0, tiled=True
        ),
    )
    neighbour_features = unpack_tiles(feature_tiles, slot_of_ref, local_blocks)
    near_prior = unpack_tiles(prior_tiles, slot_of_ref, local_blocks)
    local_features = fnorm.reshape(local_blocks, BLOCK_SAMPLES, fnorm.shape[1])
    affinity_score = jnp.einsum(
        "fwq,faq->fwa", local_features, neighbour_features, preferred_element_type=jnp.float32
    )
    edge_weight = jnp.exp(affinity_score / (FEATURE_WIDTH * SOFTMAX_HEAT)).reshape(
        local_blocks, BLOCK_SAMPLES, neighbour_count, BLOCK_SAMPLES
    )
    own_blocks = device_here * local_blocks + jnp.arange(local_blocks, dtype=jnp.int32)
    self_block = listed == own_blocks[:, None]
    block_index = jnp.arange(BLOCK_SAMPLES, dtype=jnp.int32)
    diagonal = block_index[:, None] == block_index[None, :]
    self_pair = self_block[:, None, :, None] & diagonal[None, :, None, :]
    edge_weight = jnp.where(self_pair, 0.0, edge_weight)
    prob = (edge_weight / jnp.sum(edge_weight, axis=(2, 3), keepdims=True)).astype(jnp.bfloat16)
    prob = prob.reshape(local_blocks, BLOCK_SAMPLES, neighbour_count * BLOCK_SAMPLES)
    prior_wide = prior.astype(jnp.float32)
    spread_one = jnp.einsum(
        "bik,bkc->bic", prob, near_prior, preferred_element_type=jnp.float32
    ).reshape(-1, width)
    sharp_one = jnp.square(MIXING * spread_one + (1.0 - MIXING) * prior_wide)
    label_one = (C * sharp_one / row_mass(sharp_one)[:, None]).astype(jnp.bfloat16)
    near_labels = neighbour_labels(label_one, chosen, filled, slot_of_ref, local_blocks)
    spread_two = jnp.einsum(
        "bik,bkc->bic", prob, near_labels, preferred_element_type=jnp.float32
    ).reshape(-1, width)
    sharp_two = jnp.square(MIXING * spread_two + (1.0 - MIXING) * prior_wide)
    labels = (C * sharp_two / row_mass(sharp_two)[:, None]).astype(jnp.bfloat16)
    moment = lax.psum_scatter(
        lax.dot_general(
            fnorm, labels, (((0,), (0,)), ((), ())), preferred_element_type=jnp.float32
        ).astype(jnp.bfloat16),
        "rows",
        scatter_dimension=0,
        tiled=True,
    ).astype(jnp.float32)
    squares = lax.psum(jnp.sum(moment * moment, axis=0), "rows")
    prototypes = moment / jnp.sqrt(squares / FEATURE_WIDTH + EPSILON_PROTO)[None, :]
    return (labels, prototypes)


def solution(mesh):
    placed = (P("rows", "cls"), P("rows", None), P(), P("rows"))
    return jax.shard_map(
        body,
        mesh=mesh,
        in_specs=placed,
        out_specs=(P("rows", "cls"), P("rows", "cls")),
        check_vma=False,
    )
```

profile of v0, /device:TPU:1, one launch (start us, length us, event | category | flops | bytes accessed | tf_op | source)
XLA Modules:
  0.0 695.4 jit_solution(14508505404017264798)
XLA Ops:
  12.3 3.6 gather_fusion
  15.9 6.2 select_select_fusion.2
  22.1 7.8 %all-to-all-start = ((bf16[32,128,768]{2,1,0:T(8,128)(2,1)}), bf16[32,128,768]{2,1,0:T(8,128)(2,1)}, u32[]{:S(2)}, u32[]{:S(2)}) async-start(bf16[32,128,768]{2,1,0:T(8,128)(2,1)} %select_select_fusion.2), calls=%async_computation | async-start | bytes 12582912 | tf_op jit(solution)/shard_map/all_to_all | solution.py:79
  32.3 28.1 %psum.28 = f32[512]{0:T(512)S(1)} all-reduce(f32[512]{0:T(512)S(1)} %fusion.2), channel_id=1, replica_groups=mesh['rows'=16,'cls'=16] {'cls'}, use_global_device_ids=true, to_apply=%region_6.7 | all-reduce | flops 512 | bytes 4096 | tf_op jit(solution)/shard_map/psum | solution.py:19
  64.1 6.2 gather_fusion.2
  70.3 10.2 %select_select_fusion.1 = bf16[32,128,1376]{1,2,0:T(8,128)(2,1)} fusion(bf16[32,128,1376]{1,2,0:T(8,128)(2,1)} %gather_fusion.2, pred[32]{0:T(512)(128)(4,1)S(1)} %compare_and_fusion.1, pred[32]{0:T(512)(128)(4,1)S(1)} %broadcast_in_dim.116), kind=kLoop, calls=%fused_computation.7 | loop fusion | flops 11272192 | bytes 22544448 | tf_op jit(solution)/shard_map/jit(_where)/select_n | solution.py:45
  80.5 41.6 %all-to-all-done = bf16[32,128,768]{2,1,0:T(8,128)(2,1)} async-done(((bf16[32,128,768]{2,1,0:T(8,128)(2,1)}), bf16[32,128,768]{2,1,0:T(8,128)(2,1)}, u32[]{:S(2)}, u32[]{:S(2)}) %all-to-all-start) | async-done | bytes 6291488 | tf_op jit(solution)/shard_map/all_to_all | solution.py:79
  122.1 5.4 all-to-all-start.1
  129.8 5.7 gather_fusion.1
  139.4 150.4 %all-to-all-done.1 = bf16[32,128,1376]{1,2,0:T(8,128)(2,1)} async-done(((bf16[32,128,1376]{1,2,0:T(8,128)(2,1)}), bf16[32,128,1376]{1,2,0:T(8,128)(2,1)}, u32[]{:S(2)}, u32[]{:S(2)}) %all-to-all-start.1) | async-done | bytes 11272224 | tf_op jit(solution)/shard_map/all_to_all | solution.py:82
  289.8 9.2 %gather_fusion.3 = bf16[20,128,1376]{1,2,0:T(8,128)(2,1)} fusion(bf16[32,128,1376]{1,2,0:T(8,128)(2,1)} %all-to-all-done.1, s32[1024]{0:T(1024)S(1)} %pad_clamp_fusion), kind=kCustom, calls=%fused_computation.1.clone | custom fusion | bytes 14090320 | tf_op jit(solution)/shard_map/jit(_take)/gather | solution.py:49
  299.0 6.7 broadcast_select_fusion
  305.7 9.9 %copy.103 = bf16[20,128,1376]{2,1,0:T(8,128)(2,1)} copy(bf16[20,128,1376]{1,2,0:T(8,128)(2,1)} %broadcast_select_fusion) | data formatting | bytes 14090240 | tf_op jit(solution)/shard_map/jit(_take)/select_n | solution.py:49
  315.6 7.2 %convolution_multiply_fusion.1 = f32[4,128,1376]{1,2,0:T(8,128)} fusion(bf16[4,640,1376]{2,1,0:T(8,128)(2,1)} %bitcast.58, f32[4,128,640]{2,1,0:T(8,128)S(1)} %fusion.8), kind=kOutput, calls=%fused_computation.13 | convolution fusion | flops 903136384 | bytes 11173888 | tf_op jit(solution)/shard_map/bik,bkc->bic/dot_general | solution.py:104
  322.8 3.5 copy.105
  326.3 3.5 fusion.3
  329.7 29.6 %psum.29 = f32[512]{0:T(512)} all-reduce(f32[512]{0:T(512)} %fusion.3), channel_id=1, replica_groups=mesh['rows'=16,'cls'=16] {'cls'}, use_global_device_ids=true, to_apply=%region_8.11 | all-reduce | flops 512 | bytes 4096 | tf_op jit(solution)/shard_map/psum | solution.py:19
  359.3 3.7 divide_convert_fusion.1
  364.9 6.4 gather_fusion.4
  371.3 6.4 select_select_fusion
  377.7 131.6 %all_to_all.15 = bf16[32,128,1376]{1,2,0:T(8,128)(2,1)} all-to-all(bf16[32,128,1376]{1,2,0:T(8,128)(2,1)S(1)} %select_select_fusion), channel_id=1, replica_groups=mesh['rows'=16,'cls'=16] {'rows'}, dimensions={0} | all-to-all | bytes 22544384 | tf_op jit(solution)/shard_map/all_to_all | solution.py:54
  509.3 9.3 %gather_fusion.5 = bf16[20,128,1376]{1,2,0:T(8,128)(2,1)} fusion(bf16[32,128,1376]{1,2,0:T(8,128)(2,1)} %all_to_all.15, s32[1024]{0:T(1024)} %copy-done.10), kind=kCustom, calls=%fused_computation.3.clone | custom fusion | bytes 14090320 | tf_op jit(solution)/shard_map/jit(_take)/gather | solution.py:49
  518.7 6.7 broadcast_select_fusion.1
  525.3 9.9 %copy.107 = bf16[20,128,1376]{2,1,0:T(8,128)(2,1)} copy(bf16[20,128,1376]{1,2,0:T(8,128)(2,1)} %broadcast_select_fusion.1) | data formatting | bytes 14090240 | tf_op jit(solution)/shard_map/jit(_take)/select_n | solution.py:49
  535.2 7.2 %convolution_multiply_fusion = f32[4,128,1376]{1,2,0:T(8,128)} fusion(bf16[4,640,1376]{2,1,0:T(8,128)(2,1)} %bitcast.57, f32[4,128,640]{2,1,0:T(8,128)S(1)} %fusion.8), kind=kOutput, calls=%fused_computation.12 | convolution fusion | flops 903136384 | bytes 11173888 | tf_op jit(solution)/shard_map/bik,bkc->bic/dot_general | solution.py:110
  542.4 3.5 copy.109
  545.9 2.9 fusion.4
  548.8 24.7 %psum.30 = f32[512]{0:T(512)S(1)} all-reduce(f32[512]{0:T(512)S(1)} %fusion.4), channel_id=1, replica_groups=mesh['rows'=16,'cls'=16] {'cls'}, use_global_device_ids=true, to_apply=%region_10.13 | all-reduce | flops 512 | bytes 4096 | tf_op jit(solution)/shard_map/psum | solution.py:19
  573.4 2.8 divide_convert_fusion
  577.3 2.8 convolution_convert_fusion
  583.0 71.2 %reduce-scatter.4.cloned.1.call-done = bf16[48,1376]{1,0:T(8,128)(2,1)} async-done(((bf16[768,1376]{1,0:T(8,128)(2,1)}), bf16[48,1376]{1,0:T(8,128)(2,1)}) %reduce-scatter.4.cloned.1.call-update) | async-done | bytes 132112
  655.1 31.8 %psum.31 = f32[1376]{0:T(1024)S(1)} all-reduce(f32[1376]{0:T(1024)S(1)} %fusion.10), channel_id=1, replica_groups=mesh['rows'=16,'cls'=16] {'rows'}, use_global_device_ids=true, to_apply=%region_13.16 | all-reduce | flops 1376 | bytes 11008 | tf_op jit(solution)/shard_map/psum | solution.py:123
  (86 shorter events, 25.6 us)
Async XLA Ops:
  9.3 61.1 %copy-start.11 = (pred[32]{0:T(512)(128)(4,1)}, pred[32]{0:T(512)(128)(4,1)S(1)}, u32[]{:S(2)}) copy-start(pred[32]{0:T(512)(128)(4,1)S(1)} %compare_and_fusion.1) | copy-start | bytes 100
  9.5 60.8 %copy-start.7 = (pred[32]{0:T(512)(128)(4,1)}, pred[32]{0:T(512)(128)(4,1)S(1)}, u32[]{:S(2)}) copy-start(pred[32]{0:T(512)(128)(4,1)S(1)} %broadcast_in_dim.116) | copy-start | bytes 100
  22.1 9.6 %copy-start.5 = (s32[512]{0:T(512)S(1)}, s32[512]{0:T(512)}, u32[]{:S(2)}) copy-start(s32[512]{0:T(512)} %param.11) | copy-start | bytes 6148
  22.1 100.1 %all-to-all-start = ((bf16[32,128,768]{2,1,0:T(8,128)(2,1)}), bf16[32,128,768]{2,1,0:T(8,128)(2,1)}, u32[]{:S(2)}, u32[]{:S(2)}) async-start(bf16[32,128,768]{2,1,0:T(8,128)(2,1)} %select_select_fusion.2), calls=%async_computation | async-start | bytes 12582912 | tf_op jit(solution)/shard_map/all_to_all | solution.py:79
  31.6 30.6 %copy-start = (bf16[512,1376]{1,0:T(8,128)(2,1)}, bf16[512,1376]{1,0:T(8,128)(2,1)S(1)}, u32[]{:S(2)}) copy-start(bf16[512,1376]{1,0:T(8,128)(2,1)S(1)} %copy.101) | copy-start | bytes 4227076
  64.1 6.2 copy-start.9
  80.5 48.7 %copy-start.6 = (s32[64,5]{0,1:T(8,128)S(1)}, s32[64,5]{0,1:T(8,128)}, u32[]{:S(2)}) copy-start(s32[64,5]{0,1:T(8,128)} %param.10) | copy-start | bytes 3844
  122.1 167.7 %all-to-all-start.1 = ((bf16[32,128,1376]{1,2,0:T(8,128)(2,1)}), bf16[32,128,1376]{1,2,0:T(8,128)(2,1)}, u32[]{:S(2)}, u32[]{:S(2)}) async-start(bf16[32,128,1376]{1,2,0:T(8,128)(2,1)} %select_select_fusion.1), calls=%async_computation.1 | async-start | bytes 22544384 | tf_op jit(solution)/shard_map/all_to_all | solution.py:82
  127.6 526.6 %reduce-scatter.4.cloned.1.call-start = ((), (), s32[]{:S(2)}) async-start(), calls=%async_computation.4 | async-start | bytes 2297856
  129.8 160.1 %copy-start.10 = (s32[1024]{0:T(1024)}, s32[1024]{0:T(1024)S(1)}, u32[]{:S(2)}) copy-start(s32[1024]{0:T(1024)S(1)} %pad_clamp_fusion) | copy-start | bytes 12292
  129.8 169.2 %copy-start.13 = (pred[20]{0:T(512)(128)(4,1)}, pred[20]{0:T(512)(128)(4,1)S(1)}, u32[]{:S(2)}) copy-start(pred[20]{0:T(512)(128)(4,1)S(1)} %compare_and_fusion) | copy-start | bytes 64
  322.8 3.5 copy-start.1
  364.8 6.5 copy-start.8
  364.9 6.5 copy-start.12
  509.3 9.3 %copy-start.14 = (pred[20]{0:T(512)(128)(4,1)S(1)}, pred[20]{0:T(512)(128)(4,1)}, u32[]{:S(2)}) copy-start(pred[20]{0:T(512)(128)(4,1)} %copy-done.13) | copy-start | bytes 64
  542.4 3.5 copy-start.2
  576.2 1.1 copy-start.3
  580.1 1.4 copy-start.4
Sparse Core Ops, SparseCore 0:
  580.2 73.8 reduce-scatter.3
where the time goes:
time: 704 us; the launch traced here: 695 us
  waiting for transfers between devices  263 us (37%)
  blocking collectives  246 us (35%)
  local copies, waits for them, and re-layouts  79.4 us (11%)
  other arithmetic  60.9 us (9%)
  matrix products  18.4 us (3%)
  between operations  14.4 us (2%)
  starting transfers between devices  13.4 us (2%)
    all_to_all x1, waiting for transfers between devices, body(): lax.all_to_all(pack_tiles(prior, chosen, filled), 'rows', split_axis=0, c...  150 us
    all_to_all x1, blocking collectives, neighbour_labels(): lax.all_to_all(pack_tiles(data, chosen, filled), 'rows', split_axis=0, co...  132 us
    psum x3, blocking collectives, row_mass(): return lax.psum(jnp.sum(values, axis=1), 'cls')  82.3 us
    unnamed x2, waiting for transfers between devices  71.2 us
    all_to_all x1, waiting for transfers between devices, body(): lax.all_to_all(pack_tiles(fnorm, chosen, filled), 'rows', split_axis=0, c...  41.6 us
    psum x1, blocking collectives, body(): squares = lax.psum(jnp.sum(moment * moment, axis=0), 'rows')  31.8 us
    gather x3, local copies, waits for them, and re-layouts, unpack_tiles(): picked = jnp.take(received, slot_of_ref, axis=0)  24.3 us
    select_n x3, other arithmetic, pack_tiles(): return jnp.where(filled[:, None, None], tiles, jnp.zeros_like(tiles))  22.8 us
  transfers between devices with their start and end apart: 3, of which 3 were waited for; matrix products, arithmetic and copies ran while one was open for 5% of the time, Pallas kernels for 0%

commit v1 on v0

v1 whole, which is shorter than its diff:
```python
import functools

import jax
import jax.numpy as jnp
from jax import lax
from jax.experimental import pallas as pl
from jax.experimental.pallas import tpu as pltpu
from jax.sharding import PartitionSpec as P

C = 22016
FEATURE_WIDTH = 768
BLOCK = 128
NEAR = 5
BOOST_FACTOR = 20.0
MIXING = 0.5
SOFTMAX_HEAT = 0.02
EPSILON_FEATURE = 1e-05
EPSILON_PROTO = 1e-06

ROWS = 16
CLS = 16
SIDE = 4
BPD = 4
NBLK = ROWS * BPD
WIDTH = C // CLS
PART = 96
PADDED = ROWS * PART
FSLICE = FEATURE_WIDTH // ROWS
HALF = BLOCK // 2

F32 = jnp.float32
BF16 = jnp.bfloat16


def place(g):
    q, r = lax.rem(g, BPD), lax.div(g, BPD)
    y, x = lax.div(r, SIDE), lax.rem(r, SIDE)
    odd = lax.rem(q, 2)
    return q * ROWS + r + odd * (x * SIDE + y - r)


def remote(src, dst, send, recv, **target):
    return pltpu.make_async_remote_copy(
        src_ref=src,
        dst_ref=dst,
        send_sem=send,
        recv_sem=recv,
        device_id=target,
        device_id_type=pl.DeviceIdType.MESH,
    )


class Exchange:
    def __init__(self, axis, src, dst, send, recv):
        self.axis, self.src, self.dst, self.send, self.recv = axis, src, dst, send, recv
        self.me = lax.axis_index(axis)

    def copy(self, k, slot):
        return remote(
            self.src(k), self.dst(slot), self.send.at[k], self.recv.at[slot], **{self.axis: k}
        )

    def peers(self, act):
        def step(i, carry):
            act(lax.rem(self.me + i, 16))
            return carry

        lax.fori_loop(1, 16, step, 0)

    def start(self):
        self.peers(lambda k: self.copy(k, self.me).start())

    def wait_recv(self):
        self.peers(lambda k: self.copy(k, k).wait_recv())

    def wait_send(self):
        self.peers(lambda k: self.copy(k, k).wait_send())


def kernel(
    nb, wl, s_hbm, f_hbm, lab_out, proto_out,
    s_v, f_v, fn, boosted, psend, prior, prob, inv, sharp, lab1, lab2, labrecv, acc, psb, prv,
    m0, m0r, ma, mar, mb, mbr, mc, na, nar, nbm, nbr, nc,
    loc, f1s, f1r, f1bs, f1br, f2s, f2r, f2bs, f2br, cs1, cr1, cs2, cr2,
    prs, prr, lbs, lbr, pts, ptr, m0s_, m0r_, mass, masr,
):
    me_r, me_c = lax.axis_index("rows"), lax.axis_index("cls")
    y, x = lax.div(me_r, SIDE), lax.rem(me_r, SIDE)
    core = lax.rem(me_c, 2)
    mate = me_c + 1 - 2 * core

    load_f = pltpu.make_async_copy(f_hbm, f_v, loc.at[0])
    load_f.start()
    load_s = pltpu.make_async_copy(s_hbm, s_v, loc.at[1])
    load_s.start()

    barrier = pltpu.get_barrier_semaphore()

    def greet(i, carry):
        for axis, me in (("rows", me_r), ("cls", me_c)):
            pl.semaphore_signal(
                barrier, inc=1, device_id={axis: lax.rem(me + i, 16)},
                device_id_type=pl.DeviceIdType.MESH,
            )
        return carry

    lax.fori_loop(1, 16, greet, 0)

    load_f.wait()
    for q in range(BPD):
        wide = f_v[q * BLOCK : (q + 1) * BLOCK, :].astype(F32)
        scale = jnp.sqrt(jnp.mean(wide * wide, axis=1, keepdims=True) + EPSILON_FEATURE)
        at = q * ROWS + (me_r if q % 2 == 0 else x * SIDE + y)
        fn[at] = (wide / scale).astype(BF16)
    pl.semaphore_wait(barrier, 30)

    sends = []

    def go(copy):
        copy.start()
        sends.append(copy)

    def spot(p, b, a):
        return (2 * core + p) * ROWS + b * SIDE + a

    def along(p, first, step):
        if (p == 0) == first:
            return y * SIDE + lax.rem(x + step + SIDE, SIDE)
        return lax.rem(y + step + SIDE, SIDE) * SIDE + x

    ab = ((x, y), (y, x))
    off = lambda v, d: lax.rem(v + d + SIDE, SIDE)
    whole = lambda at: fn.at[at]
    lower = lambda at: fn.at[at, pl.ds(0, HALF)]
    upper = lambda at: fn.at[at, pl.ds(HALF, HALF)]

    def first_copy(p, d, at):
        return remote(whole(at), whole(at), f1s.at[p, d > 0], f1r.at[p, d > 0], rows=along(p, True, d))

    f1s_, f1r_ = f1s, f1r

    def move(view, at, send, recv, to):
        return remote(view(at), view(at), send, recv, rows=to)

    for p in range(2):
        a, b = ab[p]
        own = spot(p, b, a)
        for i, d in enumerate((1, -1)):
            go(move(whole, own, f1s.at[p, i], f1r.at[p, i], along(p, True, d)))
    for p in range(2):
        a, b = ab[p]
        own = spot(p, b, a)
        for i, d in enumerate((1, -1)):
            go(move(whole, own, f2s.at[p, i, 0], f2r.at[p, i, 0], along(p, False, d)))

    load_s.wait()
    first_class = me_c * WIDTH
    for q in range(BPD):
        turned = s_v[q * BLOCK : (q + 1) * BLOCK, :].astype(F32).T
        hit = wl[q] == first_class + lax.broadcasted_iota(jnp.int32, (WIDTH, BLOCK), 0)
        up = turned * jnp.where(hit, 1.0 + BOOST_FACTOR, 1.0)
        boosted[q] = up
        m0[q : q + 1, :] = jnp.sum(up, axis=0, keepdims=True)
    x0 = Exchange("cls", lambda k: m0, lambda k: m0r.at[k], m0s_, m0r_)
    x0.start()

    def mate_block(p, j, at):
        go(remote(whole(at), whole(at), cs1.at[p, j], cr1.at[p, j], cls=mate))

    for p in range(2):
        a, b = ab[p]
        for i, d in enumerate((1, -1)):
            at = spot(p, b, off(a, -d))
            move(whole, at, f1s.at[p, i], f1r.at[p, i], along(p, True, d)).wait_recv()
            view = lower if i == 0 else upper
            go(move(view, at, f1bs.at[p, i], f1br.at[p, i], along(p, True, d)))
            for i2, d2 in enumerate((1, -1)):
                go(move(whole, at, f2s.at[p, i2, 1 + i], f2r.at[p, i2, 1 + i], along(p, False, d2)))
            mate_block(p, i, at)
    for p in range(2):
        a, b = ab[p]
        at = spot(p, b, off(a, 2))
        for i, d in enumerate((1, -1)):
            view = lower if i == 0 else upper
            move(view, at, f1bs.at[p, i], f1br.at[p, i], along(p, True, d)).wait_recv()
        for i2, d2 in enumerate((1, -1)):
            go(move(whole, at, f2s.at[p, i2, 3], f2r.at[p, i2, 3], along(p, False, d2)))
        mate_block(p, 2, at)

    x0.wait_recv()
    m0r[me_c] = m0[...]
    mass0 = jnp.sum(m0r[...], axis=0)
    for q in range(BPD):
        psend[q, 0:WIDTH, :] = (C * boosted[q] / mass0[q : q + 1, :]).astype(BF16)
        psend[q, WIDTH:PADDED, :] = jnp.zeros((PADDED - WIDTH, BLOCK), BF16)

    part = lambda ref, k: ref.at[:, pl.ds(pl.multiple_of(k * PART, PART), PART), :]
    blocks = lambda ref, k: ref.at[pl.ds(k * BPD, BPD)]
    keep = pltpu.make_async_copy(part(psend, me_r), blocks(prior, me_r), loc.at[2])
    keep.start()
    xp = Exchange("rows", lambda k: part(psend, k), lambda k: blocks(prior, k), prs, prr)

    shift = (0, -1, 1, 2)
    for n in range(4):
        for p in range(2):
            a, b = ab[p]
            for i, d in enumerate((1, -1)):
                at = spot(p, off(b, -d), off(a, shift[n]))
                move(whole, at, f2s.at[p, i, n], f2r.at[p, i, n], along(p, False, d)).wait_recv()
                view = lower if i == 0 else upper
                go(move(view, at, f2bs.at[p, i, n], f2br.at[p, i, n], along(p, False, d)))
                go(remote(whole(at), whole(at), cs2.at[p, i, n], cr2.at[p, i, n], cls=mate))
    xp.start()
    for n in range(4):
        for p in range(2):
            a, b = ab[p]
            at = spot(p, off(b, 2), off(a, shift[n]))
            for i, d in enumerate((1, -1)):
                view = lower if i == 0 else upper
                move(view, at, f2bs.at[p, i, n], f2br.at[p, i, n], along(p, False, d)).wait_recv()
            go(remote(whole(at), whole(at), cs2.at[p, 2, n], cr2.at[p, 2, n], cls=mate))
    for p in range(2):
        a, b = ab[p]
        other = lambda bb, aa: (2 * (1 - core) + p) * ROWS + bb * SIDE + aa
        for j, d in enumerate((-1, 1, 2)):
            at = other(b, off(a, d))
            remote(whole(at), whole(at), cs1.at[p, j], cr1.at[p, j], cls=mate).wait_recv()
        for n in range(4):
            for i, d in enumerate((-1, 1, 2)):
                at = other(off(b, d), off(a, shift[n]))
                remote(whole(at), whole(at), cs2.at[p, i, n], cr2.at[p, i, n], cls=mate).wait_recv()

    apart = lax.broadcasted_iota(jnp.int32, (BLOCK, BLOCK), 0) - lax.broadcasted_iota(
        jnp.int32, (BLOCK, BLOCK), 1
    )

    def prob_step(k, carry):
        for q in range(BPD):
            b = k * BPD + q
            listed = [nb[b, j] for j in range(NEAR)]
            near = jnp.concatenate([fn[place(g)] for g in listed], axis=0)
            score = lax.dot_general(
                near, fn[place(b)], (((1,), (1,)), ((), ())), preferred_element_type=F32
            )
            total = jnp.zeros((1, BLOCK), F32)
            for j, g in enumerate(listed):
                w = jnp.exp(score[j * BLOCK : (j + 1) * BLOCK] * (1.0 / (FEATURE_WIDTH * SOFTMAX_HEAT)))
                same = jnp.where(g == b, 0, BLOCK)
                w = jnp.where(apart == same, 0.0, w)
                total = total + jnp.sum(w, axis=0, keepdims=True)
                prob[b, j * BLOCK : (j + 1) * BLOCK, :] = w.astype(BF16)
            inv[k, q : q + 1, :] = MIXING / total
        return carry

    lax.fori_loop(0, ROWS, prob_step, 0)

    xp.wait_recv()
    keep.wait()

    def spread(ref, k, q):
        b = k * BPD + q
        near = jnp.concatenate([ref[nb[b, j]] for j in range(NEAR)], axis=1)
        got = jnp.dot(near, prob[b], preferred_element_type=F32)
        return jnp.square(got * inv[k, q : q + 1, :] + (1.0 - MIXING) * prior[b].astype(F32))

    def first_step(k, carry):
        for q in range(BPD):
            value = spread(prior, k, q)
            sharp[k * BPD + q] = value
            ma[k, q : q + 1, :] = jnp.sum(value, axis=0, keepdims=True)
        return carry

    lax.fori_loop(0, ROWS, first_step, 0)

    def total_mass(n, mine, inner, total, outer, full):
        e1 = Exchange("rows", lambda k: mine.at[k], lambda k: inner.at[k], mass.at[n, 0], masr.at[n, 0])
        e1.start()
        inner[me_r] = mine[me_r]
        e1.wait_recv()
        total[...] = jnp.sum(inner[...], axis=0)
        e2 = Exchange("cls", lambda k: total, lambda k: outer.at[k], mass.at[n, 1], masr.at[n, 1])
        e2.start()
        outer[me_c] = total[...]
        e2.wait_recv()
        full[me_r] = jnp.sum(outer[...], axis=0)
        e3 = Exchange("rows", lambda k: full.at[me_r], lambda k: full.at[k], mass.at[n, 2], masr.at[n, 2])
        e3.start()
        e3.wait_recv()
        return e1, e2, e3

    e = total_mass(0, ma, mar, mb, mbr, mc)

    def label_step(k, carry):
        for q in range(BPD):
            lab1[k * BPD + q] = (sharp[k * BPD + q] * (C / mc[k, q : q + 1, :])).astype(BF16)
        return carry

    lax.fori_loop(0, ROWS, label_step, 0)

    def second(k):
        for q in range(BPD):
            value = spread(lab1, k, q)
            lab2[k * BPD + q] = value.astype(BF16)
            na[k, q : q + 1, :] = jnp.sum(value, axis=0, keepdims=True)

    xl = Exchange("rows", lambda k: blocks(lab2, k), lambda k: part(labrecv, k), lbs, lbr)

    def second_step(i, carry):
        k = lax.rem(me_r + i, ROWS)
        second(k)
        xl.copy(k, me_r).start()
        return carry

    lax.fori_loop(1, ROWS, second_step, 0)
    second(me_r)
    keep2 = pltpu.make_async_copy(blocks(lab2, me_r), part(labrecv, me_r), loc.at[3])
    keep2.start()
    e += total_mass(1, na, nar, nbm, nbr, nc)

    acc[...] = jnp.zeros_like(acc)

    def moment_step(k, carry):
        labs = [
            (lab2[k * BPD + q].astype(F32) * (C / nc[k, q : q + 1, :])).astype(BF16)
            for q in range(BPD)
        ]
        feats = [fn[place(k * BPD + q)] for q in range(BPD)]
        acc[...] += jnp.dot(
            jnp.concatenate(labs, axis=1), jnp.concatenate(feats, axis=0), preferred_element_type=F32
        )
        return carry

    lax.fori_loop(0, ROWS, moment_step, 0)
    moment = acc[...]
    square = jnp.mean(moment * moment, axis=1, keepdims=True)
    proto = (moment / jnp.sqrt(square + EPSILON_PROTO)).T
    for k in range(ROWS):
        psb[k] = proto[k * FSLICE : (k + 1) * FSLICE, :]
    xt = Exchange("rows", lambda k: psb.at[k], lambda k: prv.at[k], pts, ptr)
    xt.start()
    prv[me_r] = psb[me_r]

    xl.wait_recv()
    keep2.wait()
    for q in range(BPD):
        value = labrecv[q, 0:WIDTH, :].astype(F32) * (C / nc[me_r, q : q + 1, :])
        lab_out[q * BLOCK : (q + 1) * BLOCK, :] = value.T.astype(BF16)
    xt.wait_recv()
    for k in range(-(-WIDTH // PART)):
        size = min(PART, WIDTH - k * PART)
        proto_out[:, k * PART : k * PART + size] = prv[k][:, 0:size]

    for copy in sends:
        copy.wait_send()
    for exchange in (x0, xp, *e, xl, xt):
        exchange.wait_send()


def body(soft_labels, features, neighbours, web_labels):
    vm, sem = pltpu.VMEM, pltpu.SemaphoreType.DMA
    mass = lambda: vm((16, BPD, BLOCK), F32)
    return pl.pallas_call(
        kernel,
        out_shape=(
            jax.ShapeDtypeStruct(soft_labels.shape, BF16),
            jax.ShapeDtypeStruct((FSLICE, WIDTH), F32),
        ),
        in_specs=[
            pl.BlockSpec(memory_space=pltpu.SMEM),
            pl.BlockSpec(memory_space=pltpu.VMEM),
            pl.BlockSpec(memory_space=pl.ANY),
            pl.BlockSpec(memory_space=pl.ANY),
        ],
        out_specs=(pl.BlockSpec(memory_space=pltpu.VMEM), pl.BlockSpec(memory_space=pltpu.VMEM)),
        scratch_shapes=[
            vm((BPD * BLOCK, WIDTH), BF16),
            vm((BPD * BLOCK, FEATURE_WIDTH), BF16),
            vm((NBLK, BLOCK, FEATURE_WIDTH), BF16),
            vm((BPD, WIDTH, BLOCK), F32),
            vm((BPD, PADDED, BLOCK), BF16),
            vm((NBLK, PART, BLOCK), BF16),
            vm((NBLK, NEAR * BLOCK, BLOCK), BF16),
            mass(),
            vm((NBLK, PART, BLOCK), F32),
            vm((NBLK, PART, BLOCK), BF16),
            vm((NBLK, PART, BLOCK), BF16),
            vm((BPD, PADDED, BLOCK), BF16),
            vm((PART, FEATURE_WIDTH), F32),
            vm((ROWS, FSLICE, PART), F32),
            vm((ROWS, FSLICE, PART), F32),
            vm((BPD, BLOCK), F32),
            mass(),
            mass(), mass(), vm((BPD, BLOCK), F32), mass(), mass(),
            mass(), mass(), vm((BPD, BLOCK), F32), mass(), mass(),
            sem((4,)),
            sem((2, 2)), sem((2, 2)), sem((2, 2)), sem((2, 2)),
            sem((2, 2, 4)), sem((2, 2, 4)), sem((2, 2, 4)), sem((2, 2, 4)),
            sem((2, 3)), sem((2, 3)), sem((2, 3, 4)), sem((2, 3, 4)),
            sem((16,)), sem((16,)), sem((16,)), sem((16,)), sem((16,)), sem((16,)),
            sem((16,)), sem((16,)),
            sem((2, 3, 16)), sem((2, 3, 16)),
        ],
        compiler_params=pltpu.CompilerParams(
            collective_id=0, has_side_effects=True, vmem_limit_bytes=58 * 2**20
        ),
    )(neighbours, web_labels.reshape(BPD, 1, BLOCK), soft_labels, features)


def solution(mesh):
    placed = (P("rows", "cls"), P("rows", None), P(), P("rows"))
    return jax.shard_map(
        body,
        mesh=mesh,
        in_specs=placed,
        out_specs=(P("rows", "cls"), P("rows", "cls")),
        check_vma=False,
    )
```

time: 704 us -> 156 us (0.22); the launches traced: 695 us -> 156 us
  waiting for transfers between devices: 263 us -> 0 us
  blocking collectives: 246 us -> 0 us
  Pallas kernels: 0 us -> 148 us
  local copies, waits for them, and re-layouts: 79.4 us -> 7.18 us
  other arithmetic: 60.9 us -> 0 us
  matrix products: 18.4 us -> 0 us
  between operations: 14.4 us -> 0.65 us
  starting transfers between devices: 13.4 us -> 0 us
    all_to_all x2 -> x0, waiting for transfers between devices: 192 us -> none  [the longest x1 150 us: body(): lax.all_to_all(pack_tiles(prior, chosen, filled), 'rows', split_axis=0, c...]
    pallas_call x0 -> x1, Pallas kernels: none -> 148 us  [body(): pl.pallas_call(kernel, out_shape=(jax.ShapeDtypeStruct(soft_labels.shape,...]
    all_to_all x1 -> x0, blocking collectives: 132 us -> none  [neighbour_labels(): lax.all_to_all(pack_tiles(data, chosen, filled), 'rows', split_axis=0, co...]
    psum x4 -> x0, blocking collectives: 114 us -> none  [the longest x3 82.3 us: row_mass(): return lax.psum(jnp.sum(values, axis=1), 'cls')]
    unnamed x2 -> x0, waiting for transfers between devices: 71.2 us -> none
    gather x6 -> x0, local copies, waits for them, and re-layouts: 40.5 us -> none  [the longest x3 24.3 us: unpack_tiles(): picked = jnp.take(received, slot_of_ref, axis=0)]
    select_n x11 -> x0, other arithmetic: 38.6 us -> none  [the longest x3 22.8 us: pack_tiles(): return jnp.where(filled[:, None, None], tiles, jnp.zeros_like(tiles))]
    select_n x3 -> x0, local copies, waits for them, and re-layouts: 19.9 us -> none  [the longest x2 19.8 us: unpack_tiles(): picked = jnp.take(received, slot_of_ref, axis=0)]
  transfers between devices with their start and end apart: 3 -> 0, of which waited for: 3 -> 0; matrix products, arithmetic and copies ran while one was open for 5% -> 0% of each run, Pallas kernels for 0% -> 0%
where the time goes in v1:
time: 156 us
  Pallas kernels  148 us (95%)
  local copies, waits for them, and re-layouts  7.18 us (5%)
    pallas_call x1, Pallas kernels, body(): pl.pallas_call(kernel, out_shape=(jax.ShapeDtypeStruct(soft_labels.shape,...  148 us
    unnamed x5, local copies, waits for them, and re-layouts  4.63 us

profile of v1, /device:TPU:1, one launch (start us, length us, event | category | flops | bytes accessed | tf_op | source)
XLA Modules:
  0.0 155.9 jit_solution(9073487040214090412)
XLA Ops:
  0.6 1.4 copy.6.nb
  2.0 2.5 %copy.7.s_hbm = bf16[512,1376]{1,0:T(8,128)(2,1)} copy(bf16[512,1376]{0,1:T(8,128)(2,1)} %param.4) | data formatting | bytes 2818048 | tf_op args[0]
  4.6 148.1 %shard_map.59 = (bf16[512,1376]{1,0:T(8,128)(2,1)}, f32[48,1376]{1,0:T(8,128)}) custom-call(s32[64,5]{1,0:T(8,128)} %copy.6.nb, s32[4,1,128]{2,1,0:T(1,128)} %bitcast.1, bf16[512,1376]{1,0:T(8,128)(2,1)} %copy.7.s_hbm, bf16[512,768]{1,0:T(8,128)(2,1)} %f_hbm.1), custom_call_target="tpu_custom_call" | custom-call | tf_op jit(solution)/shard_map/pallas_call | solution.py:362
  152.7 0.0 copy-start
  152.7 2.6 %copy.8 = bf16[512,1376]{0,1:T(8,128)(2,1)} copy(bf16[512,1376]{1,0:T(8,128)(2,1)} %get-tuple-element.2) | data formatting | bytes 2818048 | tf_op jit(solution)/shard_map/pallas_call | solution.py:362
  155.2 0.0 copy-done
  155.2 0.7 copy.10
Async XLA Ops:
  152.7 2.6 %copy-start = (f32[48,1376]{1,0:T(8,128)S(1)}, f32[48,1376]{1,0:T(8,128)}, u32[]{:S(2)}) copy-start(f32[48,1376]{1,0:T(8,128)} %get-tuple-element.7) | copy-start | bytes 792580

commit v2 on v1

v2 whole, which is shorter than its diff:
```python
import functools

import jax
import jax.numpy as jnp
from jax import lax
from jax.experimental import pallas as pl
from jax.experimental.pallas import tpu as pltpu
from jax.sharding import PartitionSpec as P

C = 22016
FEATURE_WIDTH = 768
BLOCK = 128
NEAR = 5
BOOST_FACTOR = 20.0
MIXING = 0.5
SOFTMAX_HEAT = 0.02
EPSILON_FEATURE = 1e-05
EPSILON_PROTO = 1e-06

ROWS = 16
CLS = 16
SIDE = 4
BPD = 4
NBLK = ROWS * BPD
PIECE = 32
WIDTH = C // CLS
PART = 96
PADDED = ROWS * PART
USED = -(-WIDTH // PART)
AT_ONCE, BESIDE, LATER = 6, 13, 16
FSLICE = FEATURE_WIDTH // ROWS
TAKE, MISS = 80, 48

F32 = jnp.float32
BF16 = jnp.bfloat16


def place(g):
    q, r = lax.rem(g, BPD), lax.div(g, BPD)
    y, x = lax.div(r, SIDE), lax.rem(r, SIDE)
    odd = lax.rem(q, 2)
    return q * ROWS + r + odd * (x * SIDE + y - r)


def remote(src, dst, send, recv, **target):
    return pltpu.make_async_remote_copy(
        src_ref=src,
        dst_ref=dst,
        send_sem=send,
        recv_sem=recv,
        device_id=target,
        device_id_type=pl.DeviceIdType.MESH,
    )


def wrap(v, n):
    return jnp.where(v >= n, v - n, v)


class Exchange:
    def __init__(self, axis, src, dst, send, recv, takers=16, givers=16):
        self.axis, self.src, self.dst, self.send, self.recv = axis, src, dst, send, recv
        self.takers, self.givers = takers, givers
        self.me = lax.axis_index(axis)

    def copy(self, k, slot):
        return remote(
            self.src(k), self.dst(slot), self.send.at[k], self.recv.at[slot], **{self.axis: k}
        )

    def peers(self, act, mine, other):
        def step(i, carry):
            k = wrap(self.me + i, 16)
            if mine < 16 or other < 16:
                pl.when((self.me < mine) & (k < other))(lambda: act(k))
            else:
                act(k)
            return carry

        lax.fori_loop(1, 16, step, 0)

    def start_one(self, k):
        if self.takers < 16 or self.givers < 16:
            pl.when((self.me < self.givers) & (k < self.takers))(lambda: self.copy(k, self.me).start())
        else:
            self.copy(k, self.me).start()

    def start(self):
        self.peers(lambda k: self.copy(k, self.me).start(), self.givers, self.takers)

    def wait_recv(self):
        self.peers(lambda k: self.copy(k, k).wait_recv(), self.takers, self.givers)

    def wait_send(self):
        self.peers(lambda k: self.copy(k, k).wait_send(), self.givers, self.takers)


def kernel(
    nb, wl, s_hbm, f_hbm, lab_out, scale_out, proto_out,
    s_v, f_v, fn, boosted, psend, prior, prob, inv, sharp, lab1, lab2, acc, psb, prv,
    m0, m0r, ma, mar, mb, mbr, mc, na, nar, nbm, nbr, nc,
    loc, f1s, f1r, f2s, f2r, f2bs, f2br, cs, cr, zs, zr, mzs, mzr,
    prs, prr, lbs, lbr, pts, ptr, m0s_, m0r_, mass, masr, pbs, pbr,
):
    me_r, me_c = lax.axis_index("rows"), lax.axis_index("cls")
    y, x = lax.div(me_r, SIDE), lax.rem(me_r, SIDE)
    core = lax.rem(me_c, 2)
    mate = me_c + 1 - 2 * core

    load_f = pltpu.make_async_copy(f_hbm, f_v, loc.at[0])
    load_f.start()
    load_s = pltpu.make_async_copy(s_hbm, s_v, loc.at[1])
    load_s.start()

    barrier = pltpu.get_barrier_semaphore()

    for i in range(1, 16):
        for axis, me in (("rows", me_r), ("cls", me_c)):
            pl.semaphore_signal(
                barrier, inc=1, device_id={axis: wrap(me + i, 16)}, device_id_type=pl.DeviceIdType.MESH
            )

    load_f.wait()
    for q in range(BPD):
        at = q * ROWS + (me_r if q % 2 == 0 else x * SIDE + y)
        for t in range(0, BLOCK, PIECE):
            wide = f_v[q * BLOCK + t : q * BLOCK + t + PIECE, :].astype(F32)
            scale = jnp.sqrt(jnp.mean(wide * wide, axis=1, keepdims=True) + EPSILON_FEATURE)
            fn[at, t : t + PIECE, :] = (wide * (1.0 / scale)).astype(BF16)
    pl.semaphore_wait(barrier, 30)

    sends = []

    def go(copy):
        copy.start()
        sends.append(copy)

    def move(ref, send, recv, **to):
        return remote(ref, ref, send, recv, **to)

    odd_z = lax.rem(lax.div(me_c, 2), 2)
    taken = pl.multiple_of(odd_z * MISS, 16)
    shown = odd_z * TAKE
    lacked = TAKE - shown

    def spot(p, b, a, c=core):
        return (2 * c + p) * ROWS + b * SIDE + a

    def along(p, first, step):
        if (p == 0) == first:
            return y * SIDE + wrap(x + (step + SIDE) % SIDE, SIDE)
        return wrap(y + (step + SIDE) % SIDE, SIDE) * SIDE + x

    ab = ((x, y), (y, x))
    off = lambda v, d: wrap(v + (d + SIDE) % SIDE, SIDE)
    whole = lambda at: fn.at[at, pl.ds(taken, TAKE)]
    side = lambda at: fn.at[at, pl.ds(pl.multiple_of(lacked, 16), MISS)]
    z_to = (wrap(me_c + 2, 16), wrap(me_c + 14, 16))
    both = ((0, 1), (1, -1))
    steps = (-1, 1, 2)
    shift = (0, -1, 1, 2)

    def z_send(at, n, i):
        piece = fn.at[at, pl.ds(pl.multiple_of(shown, 16), MISS)]
        go(move(piece, zs.at[n], zr.at[n], cls=z_to[i % 2]))

    def z_wait(at, n):
        move(side(at), zs.at[n], zr.at[n], cls=z_to[0]).wait_recv()

    def second_axis(p, n, at):
        for i, d in both:
            go(move(whole(at), f2s.at[p, i, n], f2r.at[p, i, n], rows=along(p, False, d)))

    def to_mate(view, at, sends_, recvs, n):
        go(move(view(at), sends_.at[n], recvs.at[n], cls=mate))

    row = lambda p, b, c=core: pl.ds(spot(p, b, 0, c), SIDE)
    first_n = lambda p, j: p * 3 + j
    second_n = lambda p, j, n: 6 + p * 12 + n * 3 + j
    row_n = lambda p, j: 6 + p * 3 + j

    for p in range(2):
        a, b = ab[p]
        own = spot(p, b, a)
        for i, d in enumerate((1, -1, 2)):
            go(move(whole(own), f1s.at[p, i], f1r.at[p, i], rows=along(p, True, d)))
    for p in range(2):
        a, b = ab[p]
        second_axis(p, 0, spot(p, b, a))

    load_s.wait()
    ahead = (
        wl[...] - me_c * WIDTH - lax.broadcasted_iota(jnp.int32, (PIECE, BPD * BLOCK), 0)
    )

    def boost(t, carry):
        at = pl.ds(pl.multiple_of(t * PIECE, PIECE), PIECE)
        up = s_v[at, :].astype(F32) * jnp.where(ahead == t * PIECE, 1.0 + BOOST_FACTOR, 1.0)
        boosted[at, :] = up
        return carry + jnp.sum(up.reshape(PIECE // 8, 8, BPD * BLOCK), axis=0)

    sums = lax.fori_loop(0, WIDTH // PIECE, boost, jnp.zeros((8, BPD * BLOCK), F32))
    m0[...] = jnp.sum(sums, axis=0, keepdims=True)
    x0 = Exchange("cls", lambda k: m0, lambda k: m0r.at[k], m0s_, m0r_)
    x0.start()

    for i, d in enumerate((1, -1, 2)):
        for p in range(2):
            a, b = ab[p]
            at = spot(p, b, off(a, -d))
            move(whole(at), f1s.at[p, i], f1r.at[p, i], rows=along(p, True, d)).wait_recv()
            second_axis(p, 1 + i, at)
            z_send(at, first_n(p, i), i + p)
            to_mate(whole, at, cs, cr, first_n(p, i))

    def second_arrivals(n):
        for p in range(2):
            a, b = ab[p]
            for i, d in both:
                at = spot(p, off(b, -d), off(a, shift[n]))
                move(whole(at), f2s.at[p, i, n], f2r.at[p, i, n], rows=along(p, False, d)).wait_recv()
                if i == n % 2:
                    go(move(whole(at), f2bs.at[p, n], f2br.at[p, n], rows=along(p, False, d)))
                z_send(at, second_n(p, i, n), n + p)

    second_arrivals(0)

    x0.wait_recv()
    m0r[me_c] = m0[...]
    over = 1.0 / jnp.sum(m0r[...], axis=0)

    def scale_prior(t, carry):
        at = pl.ds(pl.multiple_of(t * PIECE, PIECE), PIECE)
        value = ((boosted[at, :] * over) * C).astype(BF16)
        for q in range(BPD):
            psend[q, at, :] = value[:, q * BLOCK : (q + 1) * BLOCK]
        return carry

    lax.fori_loop(0, WIDTH // PIECE, scale_prior, 0)
    psend[:, WIDTH:PADDED, :] = jnp.zeros((BPD, PADDED - WIDTH, BLOCK), BF16)

    part = lambda ref, k: ref.at[:, pl.ds(pl.multiple_of(k * PART, PART), PART), :]
    blocks = lambda ref, k: ref.at[pl.ds(k * BPD, BPD)]

    @pl.when(me_r >= USED)
    def _():
        prior[...] = jnp.zeros_like(prior)

    keep = pltpu.make_async_copy(part(psend, me_r), blocks(prior, me_r), loc.at[2])
    keep.start()
    xp = Exchange("rows", lambda k: part(psend, k), lambda k: blocks(prior, k), prs, prr, takers=USED)

    for n in range(1, 4):
        second_arrivals(n)
    for p in range(2):
        for i in range(2):
            to_mate(whole, row(p, off(ab[p][1], steps[i])), cs, cr, row_n(p, i))
    for n in range(4):
        for p in range(2):
            a, b = ab[p]
            at = spot(p, off(b, 2), off(a, shift[n]))
            move(whole(at), f2bs.at[p, n], f2br.at[p, n], rows=along(p, False, 1)).wait_recv()
            z_send(at, second_n(p, 2, n), n + p)
    for p in range(2):
        to_mate(whole, row(p, off(ab[p][1], 2)), cs, cr, row_n(p, 2))
    xp.start()

    for p in range(2):
        a, b = ab[p]
        for j in range(3):
            at = spot(p, b, off(a, steps[j]))
            z_wait(at, first_n(p, j))
            to_mate(side, at, mzs, mzr, first_n(p, j))
    for j in range(3):
        for p in range(2):
            a, b = ab[p]
            for n in range(4):
                z_wait(spot(p, off(b, steps[j]), off(a, shift[n])), second_n(p, j, n))
            to_mate(side, row(p, off(b, steps[j])), mzs, mzr, row_n(p, j))
    for p in range(2):
        a, b = ab[p]
        for j in range(3):
            for at, n in (
                (spot(p, b, off(a, steps[j]), 1 - core), first_n(p, j)),
                (row(p, off(b, steps[j]), 1 - core), row_n(p, j)),
            ):
                move(whole(at), cs.at[n], cr.at[n], cls=mate).wait_recv()
                move(side(at), mzs.at[n], mzr.at[n], cls=mate).wait_recv()

    apart = lax.broadcasted_iota(jnp.int32, (BLOCK, BLOCK), 0) - lax.broadcasted_iota(
        jnp.int32, (BLOCK, BLOCK), 1
    )

    def prob_step(i, carry):
        k = core * (ROWS // 2) + i
        for q in range(BPD):
            b = k * BPD + q
            listed = [nb[j, b] for j in range(NEAR)]
            near = jnp.concatenate([fn[place(g)] for g in listed], axis=0)
            score = lax.dot_general(
                near, fn[place(b)], (((1,), (1,)), ((), ())), preferred_element_type=F32
            )
            total = jnp.zeros((1, BLOCK), F32)
            for j, g in enumerate(listed):
                w = jnp.exp(score[j * BLOCK : (j + 1) * BLOCK] * (1.0 / (FEATURE_WIDTH * SOFTMAX_HEAT)))
                same = jnp.where(g == b, 0, BLOCK)
                w = jnp.where(apart == same, 0.0, w)
                total = total + jnp.sum(w, axis=0, keepdims=True)
                prob[b, j * BLOCK : (j + 1) * BLOCK, :] = w.astype(BF16)
            inv[k, q : q + 1, :] = MIXING / total
        share(i, core).start()
        return carry

    def share(i, c):
        return move(blocks(prob, c * (ROWS // 2) + i), pbs.at[i], pbr.at[i], cls=mate)

    def share_sums(c):
        return move(inv.at[pl.ds(c * (ROWS // 2), ROWS // 2)], pbs.at[ROWS // 2], pbr.at[ROWS // 2], cls=mate)

    lax.fori_loop(0, ROWS // 2, prob_step, 0)
    share_sums(core).start()

    xp.wait_recv()
    keep.wait()
    for i in range(ROWS // 2):
        share(i, 1 - core).wait_recv()
    share_sums(1 - core).wait_recv()

    def spread(ref, k, q):
        b = k * BPD + q
        near = jnp.concatenate([ref[nb[j, b]] for j in range(NEAR)], axis=1)
        got = jnp.dot(near, prob[b], preferred_element_type=F32)
        return jnp.square(got * inv[k, q : q + 1, :] + (1.0 - MIXING) * prior[b].astype(F32))

    def reduce_over_rows(n, mine, inner):
        return Exchange("rows", lambda k: mine.at[k], lambda k: inner.at[k], mass.at[n, 0], masr.at[n, 0])

    def total_mass(n, mine, inner, total, outer, full, beside=lambda: None):
        e1 = reduce_over_rows(n, mine, inner)
        inner[me_r] = mine[me_r]
        e1.wait_recv()
        total[...] = jnp.sum(inner[...], axis=0)
        e2 = Exchange("cls", lambda k: total, lambda k: outer.at[k], mass.at[n, 1], masr.at[n, 1])
        e2.start()
        beside()
        outer[me_c] = total[...]
        e2.wait_recv()
        full[me_r] = C / jnp.sum(outer[...], axis=0)
        e3 = Exchange("rows", lambda k: full.at[me_r], lambda k: full.at[k], mass.at[n, 2], masr.at[n, 2])
        e3.start()
        return e1, e2, e3

    def first(k):
        for q in range(BPD):
            value = spread(prior, k, q)
            sharp[k * BPD + q] = value
            ma[k, q : q + 1, :] = jnp.sum(value, axis=0, keepdims=True)

    x1 = reduce_over_rows(0, ma, mar)

    def first_step(i, carry):
        k = wrap(me_r + i, ROWS)
        first(k)
        x1.start_one(k)
        return carry

    lax.fori_loop(1, ROWS, first_step, 0)
    first(me_r)
    e = total_mass(0, ma, mar, mb, mbr, mc)

    def normalise(k):
        for q in range(BPD):
            lab1[k * BPD + q] = (sharp[k * BPD + q] * mc[k, q : q + 1, :]).astype(BF16)

    normalise(me_r)

    def label_step(i, carry):
        k = wrap(me_r + i, ROWS)
        e[2].copy(k, k).wait_recv()
        normalise(k)
        return carry

    lax.fori_loop(1, ROWS, label_step, 0)

    def second(k):
        for q in range(BPD):
            value = spread(lab1, k, q)
            lab2[k, :, q * BLOCK : (q + 1) * BLOCK] = value.astype(BF16)
            na[k, q : q + 1, :] = jnp.sum(value, axis=0, keepdims=True)

    landing = lambda k: lab_out.at[pl.ds(pl.multiple_of(k * PART, PART), PART)]
    xl = Exchange("rows", lambda k: lab2.at[k], landing, lbs, lbr, givers=USED)
    x2 = reduce_over_rows(1, na, nar)

    def second_step(i, carry):
        k = wrap(me_r + i, ROWS)
        second(k)
        x2.start_one(k)
        pl.when(i <= AT_ONCE)(lambda: xl.start_one(k))
        return carry

    def send_labels(first, last):
        def step(i, carry):
            xl.start_one(wrap(me_r + i, ROWS))
            return carry

        lax.fori_loop(first, last, step, 0)

    lax.fori_loop(1, ROWS, second_step, 0)
    second(me_r)
    keep2 = pltpu.make_async_copy(lab2.at[me_r], landing(me_r), loc.at[3])
    keep2.start()
    e += total_mass(1, na, nar, nbm, nbr, nc, lambda: send_labels(AT_ONCE + 1, BESIDE))
    e[5].wait_recv()
    send_labels(BESIDE, LATER)

    acc[...] = jnp.zeros_like(acc)

    def moment_of(k):
        labs = [
            (lab2[k, :, q * BLOCK : (q + 1) * BLOCK].astype(F32) * nc[k, q : q + 1, :]).astype(BF16)
            for q in range(BPD)
        ]
        feats = [fn[place(k * BPD + q)] for q in range(BPD)]
        acc[...] += jnp.dot(
            jnp.concatenate(labs, axis=1), jnp.concatenate(feats, axis=0), preferred_element_type=F32
        )

    def moment_step(k, carry):
        moment_of(k)
        return carry

    lax.fori_loop(0, ROWS, moment_step, 0)
    moment = acc[...]
    square = jnp.mean(moment * moment, axis=1, keepdims=True)
    proto = (moment / jnp.sqrt(square + EPSILON_PROTO)).T
    for k in range(ROWS):
        psb[k] = proto[k * FSLICE : (k + 1) * FSLICE, :]
    xt = Exchange("rows", lambda k: psb.at[k], lambda k: prv.at[k], pts, ptr)
    xt.start()
    send_labels(LATER, ROWS)
    prv[me_r] = psb[me_r]

    scale_out[...] = nc[me_r]
    xl.wait_recv()
    keep2.wait()
    xt.wait_recv()
    for k in range(USED):
        size = min(PART, WIDTH - k * PART)
        proto_out[:, k * PART : k * PART + size] = prv[k][:, 0:size]

    for copy in sends:
        copy.wait_send()
    for i in range(ROWS // 2):
        share(i, core).wait_send()
    share_sums(core).wait_send()
    for exchange in (x0, xp, *e, xl, xt):
        exchange.wait_send()


def body(soft_labels, features, neighbours, web_labels):
    vm, sem = pltpu.VMEM, pltpu.SemaphoreType.DMA
    mass = lambda: vm((16, BPD, BLOCK), F32)
    turned, scale, prototypes = pl.pallas_call(
        kernel,
        out_shape=(
            jax.ShapeDtypeStruct((PADDED, BPD * BLOCK), BF16),
            jax.ShapeDtypeStruct((BPD, BLOCK), F32),
            jax.ShapeDtypeStruct((FSLICE, WIDTH), F32),
        ),
        in_specs=[
            pl.BlockSpec(memory_space=pltpu.SMEM),
            pl.BlockSpec(memory_space=pltpu.VMEM),
            pl.BlockSpec(memory_space=pl.ANY),
            pl.BlockSpec(memory_space=pl.ANY),
        ],
        out_specs=(
            pl.BlockSpec(memory_space=pl.ANY),
            pl.BlockSpec(memory_space=pltpu.VMEM),
            pl.BlockSpec(memory_space=pltpu.VMEM),
        ),
        scratch_shapes=[
            vm((WIDTH, BPD * BLOCK), BF16),
            vm((BPD * BLOCK, FEATURE_WIDTH), BF16),
            vm((NBLK, BLOCK, FEATURE_WIDTH), BF16),
            vm((WIDTH, BPD * BLOCK), F32),
            vm((BPD, PADDED, BLOCK), BF16),
            vm((NBLK, PART, BLOCK), BF16),
            vm((NBLK, NEAR * BLOCK, BLOCK), BF16),
            mass(),
            vm((NBLK, PART, BLOCK), F32),
            vm((NBLK, PART, BLOCK), BF16),
            vm((ROWS, PART, BPD * BLOCK), BF16),
            vm((PART, FEATURE_WIDTH), F32),
            vm((ROWS, FSLICE, PART), F32),
            vm((ROWS, FSLICE, PART), F32),
            vm((1, BPD * BLOCK), F32),
            vm((CLS, 1, BPD * BLOCK), F32),
            mass(), mass(), vm((BPD, BLOCK), F32), mass(), mass(),
            mass(), mass(), vm((BPD, BLOCK), F32), mass(), mass(),
            sem((4,)),
            sem((2, 3)), sem((2, 3)),
            sem((2, 2, 4)), sem((2, 2, 4)), sem((2, 4)), sem((2, 4)),
            sem((12,)), sem((12,)), sem((30,)), sem((30,)), sem((12,)), sem((12,)),
            sem((16,)), sem((16,)), sem((16,)), sem((16,)), sem((16,)), sem((16,)),
            sem((16,)), sem((16,)),
            sem((2, 3, 16)), sem((2, 3, 16)),
            sem((9,)), sem((9,)),
        ],
        compiler_params=pltpu.CompilerParams(
            collective_id=0, has_side_effects=True, vmem_limit_bytes=58 * 2**20
        ),
    )(neighbours.T, web_labels.reshape(1, BPD * BLOCK), soft_labels.T, features)
    labels = (turned[:WIDTH].astype(F32) * scale.reshape(1, BPD * BLOCK)).astype(BF16)
    return labels.T, prototypes


def solution(mesh):
    placed = (P("rows", "cls"), P("rows", None), P(), P("rows"))
    return jax.shard_map(
        body,
        mesh=mesh,
        in_specs=placed,
        out_specs=(P("rows", "cls"), P("rows", "cls")),
        check_vma=False,
    )
```

time: 156 us -> 124 us (0.79)
  Pallas kernels: 148 us -> 119 us
  local copies, waits for them, and re-layouts: 7.18 us -> 0.71 us
  other arithmetic: 0 us -> 2.75 us
    pallas_call x1, Pallas kernels: 148 us -> 119 us  [body(): pl.pallas_call(kernel, out_shape=(jax.ShapeDtypeStruct((PADDED, BPD * BLO...]
    unnamed x5 -> x3, local copies, waits for them, and re-layouts: 4.63 us -> 0.71 us
    transpose x0 -> x1, other arithmetic: none -> 2.75 us  [body(): return (labels.T, prototypes)]
    pallas_call x1 -> x0, local copies, waits for them, and re-layouts: 2.55 us -> none  [body(): pl.pallas_call(kernel, out_shape=(jax.ShapeDtypeStruct(soft_labels.shape,...]
where the time goes in v2:
time: 124 us
  Pallas kernels  119 us (96%)
  other arithmetic  2.75 us (2%)
    pallas_call x1, Pallas kernels, body(): pl.pallas_call(kernel, out_shape=(jax.ShapeDtypeStruct((PADDED, BPD * BLO...  119 us
    transpose x1, other arithmetic, body(): return (labels.T, prototypes)  2.75 us

profile of v2, /device:TPU:1, one launch (start us, length us, event | category | flops | bytes accessed | tf_op | source)
XLA Modules:
  0.0 123.6 jit_solution(677028044967653801)
XLA Ops:
  0.6 119.5 %shard_map.59 = (bf16[1536,512]{1,0:T(8,128)(2,1)}, f32[4,128]{1,0:T(4,128)}, f32[48,1376]{1,0:T(8,128)}) custom-call(s32[5,64]{1,0:T(8,128)} %bitcast.7, s32[1,512]{1,0:T(1,128)} %bitcast.8, bf16[1376,512]{1,0:T(8,128)(2,1)} %bitcast.6, bf16[512,768]{1,0:T(8,128)(2,1)} %f_hbm.1), custom_call_target="tpu_custom_call" | custom-call | tf_op jit(solution)/shard_map/pallas_call | solution.py:464
  120.1 0.0 copy-start
  120.1 2.8 %fusion = bf16[512,1376]{0,1:T(8,128)(2,1)} fusion(f32[512]{0:T(512)} %bitcast.9, bf16[1536,512]{1,0:T(8,128)(2,1)} %get-tuple-element.5), kind=kLoop, calls=%fused_computation.1 | loop fusion | flops 2113536 | bytes 2820096 | tf_op jit(solution)/shard_map/transpose | solution.py:515
  122.9 0.0 copy-done
  122.9 0.7 copy.7
Async XLA Ops:
  120.1 2.8 %copy-start = (f32[48,1376]{1,0:T(8,128)S(1)}, f32[48,1376]{1,0:T(8,128)}, u32[]{:S(2)}) copy-start(f32[48,1376]{1,0:T(8,128)} %get-tuple-element.11) | copy-start | bytes 792580

commit v3 on v2

--- a/solution.py
+++ b/solution.py
@@ -27,7 +27,7 @@
 PART = 96
 PADDED = ROWS * PART
 USED = -(-WIDTH // PART)
-AT_ONCE, BESIDE, LATER = 6, 13, 16
+AT_ONCE = 6
 FSLICE = FEATURE_WIDTH // ROWS
 TAKE, MISS = 80, 48
 
@@ -188,22 +188,6 @@
         a, b = ab[p]
         second_axis(p, 0, spot(p, b, a))
 
-    load_s.wait()
-    ahead = (
-        wl[...] - me_c * WIDTH - lax.broadcasted_iota(jnp.int32, (PIECE, BPD * BLOCK), 0)
-    )
-
-    def boost(t, carry):
-        at = pl.ds(pl.multiple_of(t * PIECE, PIECE), PIECE)
-        up = s_v[at, :].astype(F32) * jnp.where(ahead == t * PIECE, 1.0 + BOOST_FACTOR, 1.0)
-        boosted[at, :] = up
-        return carry + jnp.sum(up.reshape(PIECE // 8, 8, BPD * BLOCK), axis=0)
-
-    sums = lax.fori_loop(0, WIDTH // PIECE, boost, jnp.zeros((8, BPD * BLOCK), F32))
-    m0[...] = jnp.sum(sums, axis=0, keepdims=True)
-    x0 = Exchange("cls", lambda k: m0, lambda k: m0r.at[k], m0s_, m0r_)
-    x0.start()
-
     for i, d in enumerate((1, -1, 2)):
         for p in range(2):
             a, b = ab[p]
@@ -212,6 +196,22 @@
             second_axis(p, 1 + i, at)
             z_send(at, first_n(p, i), i + p)
             to_mate(whole, at, cs, cr, first_n(p, i))
+
+    load_s.wait()
+    ahead = (
+        wl[...] - me_c * WIDTH - lax.broadcasted_iota(jnp.int32, (PIECE, BPD * BLOCK), 0)
+    )
+
+    def boost(t, carry):
+        at = pl.ds(pl.multiple_of(t * PIECE, PIECE), PIECE)
+        up = s_v[at, :].astype(F32) * jnp.where(ahead == t * PIECE, 1.0 + BOOST_FACTOR, 1.0)
+        boosted[at, :] = up
+        return carry + jnp.sum(up.reshape(PIECE // 8, 8, BPD * BLOCK), axis=0)
+
+    sums = lax.fori_loop(0, WIDTH // PIECE, boost, jnp.zeros((8, BPD * BLOCK), F32))
+    m0[...] = jnp.sum(sums, axis=0, keepdims=True)
+    x0 = Exchange("cls", lambda k: m0, lambda k: m0r.at[k], m0s_, m0r_)
+    x0.start()
 
     def second_arrivals(n):
         for p in range(2):
@@ -223,34 +223,7 @@
                     go(move(whole(at), f2bs.at[p, n], f2br.at[p, n], rows=along(p, False, d)))
                 z_send(at, second_n(p, i, n), n + p)
 
-    second_arrivals(0)
-
-    x0.wait_recv()
-    m0r[me_c] = m0[...]
-    over = 1.0 / jnp.sum(m0r[...], axis=0)
-
-    def scale_prior(t, carry):
-        at = pl.ds(pl.multiple_of(t * PIECE, PIECE), PIECE)
-        value = ((boosted[at, :] * over) * C).astype(BF16)
-        for q in range(BPD):
-            psend[q, at, :] = value[:, q * BLOCK : (q + 1) * BLOCK]
-        return carry
-
-    lax.fori_loop(0, WIDTH // PIECE, scale_prior, 0)
-    psend[:, WIDTH:PADDED, :] = jnp.zeros((BPD, PADDED - WIDTH, BLOCK), BF16)
-
-    part = lambda ref, k: ref.at[:, pl.ds(pl.multiple_of(k * PART, PART), PART), :]
-    blocks = lambda ref, k: ref.at[pl.ds(k * BPD, BPD)]
-
-    @pl.when(me_r >= USED)
-    def _():
-        prior[...] = jnp.zeros_like(prior)
-
-    keep = pltpu.make_async_copy(part(psend, me_r), blocks(prior, me_r), loc.at[2])
-    keep.start()
-    xp = Exchange("rows", lambda k: part(psend, k), lambda k: blocks(prior, k), prs, prr, takers=USED)
-
-    for n in range(1, 4):
+    for n in range(4):
         second_arrivals(n)
     for p in range(2):
         for i in range(2):
@@ -263,6 +236,31 @@
             z_send(at, second_n(p, 2, n), n + p)
     for p in range(2):
         to_mate(whole, row(p, off(ab[p][1], 2)), cs, cr, row_n(p, 2))
+    x0.wait_recv()
+    m0r[me_c] = m0[...]
+    over = 1.0 / jnp.sum(m0r[...], axis=0)
+
+    def scale_prior(t, carry):
+        at = pl.ds(pl.multiple_of(t * PIECE, PIECE), PIECE)
+        value = ((boosted[at, :] * over) * C).astype(BF16)
+        for q in range(BPD):
+            psend[q, at, :] = value[:, q * BLOCK : (q + 1) * BLOCK]
+        return carry
+
+    lax.fori_loop(0, WIDTH // PIECE, scale_prior, 0)
+    psend[:, WIDTH:PADDED, :] = jnp.zeros((BPD, PADDED - WIDTH, BLOCK), BF16)
+
+    part = lambda ref, k: ref.at[:, pl.ds(pl.multiple_of(k * PART, PART), PART), :]
+    blocks = lambda ref, k: ref.at[pl.ds(k * BPD, BPD)]
+
+    @pl.when(me_r >= USED)
+    def _():
+        prior[...] = jnp.zeros_like(prior)
+
+    keep = pltpu.make_async_copy(part(psend, me_r), blocks(prior, me_r), loc.at[2])
+    keep.start()
+    xp = Exchange("rows", lambda k: part(psend, k), lambda k: blocks(prior, k), prs, prr, takers=USED)
+
     xp.start()
 
     for p in range(2):
@@ -332,22 +330,22 @@
         got = jnp.dot(near, prob[b], preferred_element_type=F32)
         return jnp.square(got * inv[k, q : q + 1, :] + (1.0 - MIXING) * prior[b].astype(F32))
 
-    def reduce_over_rows(n, mine, inner):
-        return Exchange("rows", lambda k: mine.at[k], lambda k: inner.at[k], mass.at[n, 0], masr.at[n, 0])
+    def reduce_over_classes(n, mine, inner):
+        return Exchange("cls", lambda k: mine.at[k], lambda k: inner.at[k], mass.at[n, 0], masr.at[n, 0])
 
     def total_mass(n, mine, inner, total, outer, full, beside=lambda: None):
-        e1 = reduce_over_rows(n, mine, inner)
-        inner[me_r] = mine[me_r]
+        e1 = reduce_over_classes(n, mine, inner)
+        inner[me_c] = mine[me_c]
         e1.wait_recv()
         total[...] = jnp.sum(inner[...], axis=0)
-        e2 = Exchange("cls", lambda k: total, lambda k: outer.at[k], mass.at[n, 1], masr.at[n, 1])
+        e2 = Exchange("rows", lambda k: total, lambda k: outer.at[k], mass.at[n, 1], masr.at[n, 1])
         e2.start()
+        outer[me_r] = total[...]
+        e2.wait_recv()
+        full[me_c] = C / jnp.sum(outer[...], axis=0)
+        e3 = Exchange("cls", lambda k: full.at[me_c], lambda k: full.at[k], mass.at[n, 2], masr.at[n, 2])
+        e3.start()
         beside()
-        outer[me_c] = total[...]
-        e2.wait_recv()
-        full[me_r] = C / jnp.sum(outer[...], axis=0)
-        e3 = Exchange("rows", lambda k: full.at[me_r], lambda k: full.at[k], mass.at[n, 2], masr.at[n, 2])
-        e3.start()
         return e1, e2, e3
 
     def first(k):
@@ -356,26 +354,26 @@
             sharp[k * BPD + q] = value
             ma[k, q : q + 1, :] = jnp.sum(value, axis=0, keepdims=True)
 
-    x1 = reduce_over_rows(0, ma, mar)
+    x1 = reduce_over_classes(0, ma, mar)
 
     def first_step(i, carry):
-        k = wrap(me_r + i, ROWS)
+        k = wrap(me_c + i, ROWS)
         first(k)
         x1.start_one(k)
         return carry
 
     lax.fori_loop(1, ROWS, first_step, 0)
-    first(me_r)
+    first(me_c)
     e = total_mass(0, ma, mar, mb, mbr, mc)
 
     def normalise(k):
         for q in range(BPD):
             lab1[k * BPD + q] = (sharp[k * BPD + q] * mc[k, q : q + 1, :]).astype(BF16)
 
-    normalise(me_r)
+    normalise(me_c)
 
     def label_step(i, carry):
-        k = wrap(me_r + i, ROWS)
+        k = wrap(me_c + i, ROWS)
         e[2].copy(k, k).wait_recv()
         normalise(k)
         return carry
@@ -390,12 +388,12 @@
 
     landing = lambda k: lab_out.at[pl.ds(pl.multiple_of(k * PART, PART), PART)]
     xl = Exchange("rows", lambda k: lab2.at[k], landing, lbs, lbr, givers=USED)
-    x2 = reduce_over_rows(1, na, nar)
+    x2 = reduce_over_classes(1, na, nar)
 
     def second_step(i, carry):
         k = wrap(me_r + i, ROWS)
         second(k)
-        x2.start_one(k)
+        pl.when(k != me_c)(lambda: x2.start_one(k))
         pl.when(i <= AT_ONCE)(lambda: xl.start_one(k))
         return carry
 
@@ -408,11 +406,10 @@
 
     lax.fori_loop(1, ROWS, second_step, 0)
     second(me_r)
+    pl.when(me_r != me_c)(lambda: x2.start_one(me_r))
     keep2 = pltpu.make_async_copy(lab2.at[me_r], landing(me_r), loc.at[3])
     keep2.start()
-    e += total_mass(1, na, nar, nbm, nbr, nc, lambda: send_labels(AT_ONCE + 1, BESIDE))
-    e[5].wait_recv()
-    send_labels(BESIDE, LATER)
+    e += total_mass(1, na, nar, nbm, nbr, nc, lambda: send_labels(AT_ONCE + 1, ROWS))
 
     acc[...] = jnp.zeros_like(acc)
 
@@ -426,11 +423,15 @@
             jnp.concatenate(labs, axis=1), jnp.concatenate(feats, axis=0), preferred_element_type=F32
         )
 
-    def moment_step(k, carry):
+    moment_of(me_c)
+
+    def moment_step(i, carry):
+        k = wrap(me_c + i, ROWS)
+        e[5].copy(k, k).wait_recv()
         moment_of(k)
         return carry
 
-    lax.fori_loop(0, ROWS, moment_step, 0)
+    lax.fori_loop(1, ROWS, moment_step, 0)
     moment = acc[...]
     square = jnp.mean(moment * moment, axis=1, keepdims=True)
     proto = (moment / jnp.sqrt(square + EPSILON_PROTO)).T
@@ -438,7 +439,6 @@
         psb[k] = proto[k * FSLICE : (k + 1) * FSLICE, :]
     xt = Exchange("rows", lambda k: psb.at[k], lambda k: prv.at[k], pts, ptr)
     xt.start()
-    send_labels(LATER, ROWS)
     prv[me_r] = psb[me_r]
 
     scale_out[...] = nc[me_r]

time: 124 us -> 122 us (0.984); the launches traced: 124 us -> 119 us
  Pallas kernels: 119 us -> 115 us
    pallas_call x1, Pallas kernels: 119 us -> 115 us  [body(): pl.pallas_call(kernel, out_shape=(jax.ShapeDtypeStruct((PADDED, BPD * BLO...]
where the time goes in v3:
time: 122 us; the launch traced here: 119 us
  Pallas kernels  115 us (94%)
  other arithmetic  2.75 us (2%)
    pallas_call x1, Pallas kernels, body(): pl.pallas_call(kernel, out_shape=(jax.ShapeDtypeStruct((PADDED, BPD * BLO...  115 us
    transpose x1, other arithmetic, body(): return (labels.T, prototypes)  2.75 us

profile of v3, /device:TPU:1, one launch (start us, length us, event | category | flops | bytes accessed | tf_op | source)
XLA Modules:
  0.0 119.2 jit_solution(15093723415571860023)
XLA Ops:
  0.6 115.1 %shard_map.59 = (bf16[1536,512]{1,0:T(8,128)(2,1)}, f32[4,128]{1,0:T(4,128)}, f32[48,1376]{1,0:T(8,128)}) custom-call(s32[5,64]{1,0:T(8,128)} %bitcast.7, s32[1,512]{1,0:T(1,128)} %bitcast.8, bf16[1376,512]{1,0:T(8,128)(2,1)} %bitcast.6, bf16[512,768]{1,0:T(8,128)(2,1)} %f_hbm.1), custom_call_target="tpu_custom_call" | custom-call | tf_op jit(solution)/shard_map/pallas_call | solution.py:464
  115.8 0.0 copy-start
  115.8 2.8 %fusion = bf16[512,1376]{0,1:T(8,128)(2,1)} fusion(f32[512]{0:T(512)} %bitcast.9, bf16[1536,512]{1,0:T(8,128)(2,1)} %get-tuple-element.5), kind=kLoop, calls=%fused_computation.1 | loop fusion | flops 2113536 | bytes 2820096 | tf_op jit(solution)/shard_map/transpose | solution.py:515
  118.5 0.0 copy-done
  118.5 0.7 copy.7
Async XLA Ops:
  115.8 2.8 %copy-start = (f32[48,1376]{1,0:T(8,128)S(1)}, f32[48,1376]{1,0:T(8,128)}, u32[]{:S(2)}) copy-start(f32[48,1376]{1,0:T(8,128)} %get-tuple-element.11) | copy-start | bytes 792580

commit v4 on v3

--- a/solution.py
+++ b/solution.py
@@ -184,17 +184,16 @@
         own = spot(p, b, a)
         for i, d in enumerate((1, -1, 2)):
             go(move(whole(own), f1s.at[p, i], f1r.at[p, i], rows=along(p, True, d)))
-    for p in range(2):
-        a, b = ab[p]
-        second_axis(p, 0, spot(p, b, a))
 
     for i, d in enumerate((1, -1, 2)):
         for p in range(2):
             a, b = ab[p]
             at = spot(p, b, off(a, -d))
             move(whole(at), f1s.at[p, i], f1r.at[p, i], rows=along(p, True, d)).wait_recv()
+            z_send(at, first_n(p, i), i + p)
+            if i == 0:
+                second_axis(p, 0, spot(p, b, a))
             second_axis(p, 1 + i, at)
-            z_send(at, first_n(p, i), i + p)
             to_mate(whole, at, cs, cr, first_n(p, i))
 
     load_s.wait()
@@ -219,12 +218,46 @@
             for i, d in both:
                 at = spot(p, off(b, -d), off(a, shift[n]))
                 move(whole(at), f2s.at[p, i, n], f2r.at[p, i, n], rows=along(p, False, d)).wait_recv()
+                z_send(at, second_n(p, i, n), n + p)
                 if i == n % 2:
                     go(move(whole(at), f2bs.at[p, n], f2br.at[p, n], rows=along(p, False, d)))
-                z_send(at, second_n(p, i, n), n + p)
-
-    for n in range(4):
+
+    for n in range(2):
         second_arrivals(n)
+
+    x0.wait_recv()
+    m0r[me_c] = m0[...]
+    over = 1.0 / jnp.sum(m0r[...], axis=0)
+
+    def scale_prior(t, carry):
+        at = pl.ds(pl.multiple_of(t * PIECE, PIECE), PIECE)
+        value = ((boosted[at, :] * over) * C).astype(BF16)
+        for q in range(BPD):
+            psend[q, at, :] = value[:, q * BLOCK : (q + 1) * BLOCK]
+        return carry
+
+    lax.fori_loop(0, WIDTH // PIECE, scale_prior, 0)
+    psend[:, WIDTH:PADDED, :] = jnp.zeros((BPD, PADDED - WIDTH, BLOCK), BF16)
+
+    part = lambda ref, k: ref.at[:, pl.ds(pl.multiple_of(k * PART, PART), PART), :]
+    blocks = lambda ref, k: ref.at[pl.ds(k * BPD, BPD)]
+
+    @pl.when(me_r >= USED)
+    def _():
+        prior[...] = jnp.zeros_like(prior)
+
+    keep = pltpu.make_async_copy(part(psend, me_r), blocks(prior, me_r), loc.at[2])
+    keep.start()
+    xp = Exchange("rows", lambda k: part(psend, k), lambda k: blocks(prior, k), prs, prr, takers=USED)
+
+    for n in range(2, 4):
+        second_arrivals(n)
+    for p in range(2):
+        a, b = ab[p]
+        for j in range(3):
+            at = spot(p, b, off(a, steps[j]))
+            z_wait(at, first_n(p, j))
+            to_mate(side, at, mzs, mzr, first_n(p, j))
     for p in range(2):
         for i in range(2):
             to_mate(whole, row(p, off(ab[p][1], steps[i])), cs, cr, row_n(p, i))
@@ -236,39 +269,8 @@
             z_send(at, second_n(p, 2, n), n + p)
     for p in range(2):
         to_mate(whole, row(p, off(ab[p][1], 2)), cs, cr, row_n(p, 2))
-    x0.wait_recv()
-    m0r[me_c] = m0[...]
-    over = 1.0 / jnp.sum(m0r[...], axis=0)
-
-    def scale_prior(t, carry):
-        at = pl.ds(pl.multiple_of(t * PIECE, PIECE), PIECE)
-        value = ((boosted[at, :] * over) * C).astype(BF16)
-        for q in range(BPD):
-            psend[q, at, :] = value[:, q * BLOCK : (q + 1) * BLOCK]
-        return carry
-
-    lax.fori_loop(0, WIDTH // PIECE, scale_prior, 0)
-    psend[:, WIDTH:PADDED, :] = jnp.zeros((BPD, PADDED - WIDTH, BLOCK), BF16)
-
-    part = lambda ref, k: ref.at[:, pl.ds(pl.multiple_of(k * PART, PART), PART), :]
-    blocks = lambda ref, k: ref.at[pl.ds(k * BPD, BPD)]
-
-    @pl.when(me_r >= USED)
-    def _():
-        prior[...] = jnp.zeros_like(prior)
-
-    keep = pltpu.make_async_copy(part(psend, me_r), blocks(prior, me_r), loc.at[2])
-    keep.start()
-    xp = Exchange("rows", lambda k: part(psend, k), lambda k: blocks(prior, k), prs, prr, takers=USED)
-
     xp.start()
 
-    for p in range(2):
-        a, b = ab[p]
-        for j in range(3):
-            at = spot(p, b, off(a, steps[j]))
-            z_wait(at, first_n(p, j))
-            to_mate(side, at, mzs, mzr, first_n(p, j))
     for j in range(3):
         for p in range(2):
             a, b = ab[p]

time: 122 us -> 120 us (0.984)
  no operation moved by 1% of the time
where the time goes in v4:
time: 120 us; the launch traced here: 118 us
  Pallas kernels  114 us (95%)
  other arithmetic  2.75 us (2%)
    pallas_call x1, Pallas kernels, body(): pl.pallas_call(kernel, out_shape=(jax.ShapeDtypeStruct((PADDED, BPD * BLO...  114 us
    transpose x1, other arithmetic, body(): return (labels.T, prototypes)  2.75 us

profile of v4, /device:TPU:1, one launch (start us, length us, event | category | flops | bytes accessed | tf_op | source)
XLA Modules:
  0.0 118.0 jit_solution(12018607948181595266)
XLA Ops:
  0.6 113.9 %shard_map.59 = (bf16[1536,512]{1,0:T(8,128)(2,1)}, f32[4,128]{1,0:T(4,128)}, f32[48,1376]{1,0:T(8,128)}) custom-call(s32[5,64]{1,0:T(8,128)} %bitcast.7, s32[1,512]{1,0:T(1,128)} %bitcast.8, bf16[1376,512]{1,0:T(8,128)(2,1)} %bitcast.6, bf16[512,768]{1,0:T(8,128)(2,1)} %f_hbm.1), custom_call_target="tpu_custom_call" | custom-call | tf_op jit(solution)/shard_map/pallas_call | solution.py:466
  114.6 0.0 copy-start
  114.6 2.8 %fusion = bf16[512,1376]{0,1:T(8,128)(2,1)} fusion(f32[512]{0:T(512)} %bitcast.9, bf16[1536,512]{1,0:T(8,128)(2,1)} %get-tuple-element.5), kind=kLoop, calls=%fused_computation.1 | loop fusion | flops 2113536 | bytes 2820096 | tf_op jit(solution)/shard_map/transpose | solution.py:517
  117.3 0.0 copy-done
  117.3 0.7 copy.7
Async XLA Ops:
  114.6 2.8 %copy-start = (f32[48,1376]{1,0:T(8,128)S(1)}, f32[48,1376]{1,0:T(8,128)}, u32[]{:S(2)}) copy-start(f32[48,1376]{1,0:T(8,128)} %get-tuple-element.11) | copy-start | bytes 792580

commit v5 on v4

--- a/solution.py
+++ b/solution.py
@@ -438,8 +438,8 @@
     square = jnp.mean(moment * moment, axis=1, keepdims=True)
     proto = (moment / jnp.sqrt(square + EPSILON_PROTO)).T
     for k in range(ROWS):
-        psb[k] = proto[k * FSLICE : (k + 1) * FSLICE, :]
-    xt = Exchange("rows", lambda k: psb.at[k], lambda k: prv.at[k], pts, ptr)
+        psb[k] = proto[k * FSLICE : (k + 1) * FSLICE, :].astype(BF16)
+    xt = Exchange("rows", lambda k: psb.at[k], lambda k: prv.at[k], pts, ptr, givers=USED)
     xt.start()
     prv[me_r] = psb[me_r]
 
@@ -449,7 +449,7 @@
     xt.wait_recv()
     for k in range(USED):
         size = min(PART, WIDTH - k * PART)
-        proto_out[:, k * PART : k * PART + size] = prv[k][:, 0:size]
+        proto_out[:, k * PART : k * PART + size] = prv[k][:, 0:size].astype(F32)
 
     for copy in sends:
         copy.wait_send()
@@ -494,8 +494,8 @@
             vm((NBLK, PART, BLOCK), BF16),
             vm((ROWS, PART, BPD * BLOCK), BF16),
             vm((PART, FEATURE_WIDTH), F32),
-            vm((ROWS, FSLICE, PART), F32),
-            vm((ROWS, FSLICE, PART), F32),
+            vm((ROWS, FSLICE, PART), BF16),
+            vm((ROWS, FSLICE, PART), BF16),
             vm((1, BPD * BLOCK), F32),
             vm((CLS, 1, BPD * BLOCK), F32),
             mass(), mass(), vm((BPD, BLOCK), F32), mass(), mass(),

time: 120 us -> 118 us (0.983)
  Pallas kernels: 114 us -> 112 us
    pallas_call x1, Pallas kernels: 114 us -> 112 us  [body(): pl.pallas_call(kernel, out_shape=(jax.ShapeDtypeStruct((PADDED, BPD * BLO...]
where the time goes in v5:
time: 118 us; the launch traced here: 116 us
  Pallas kernels  112 us (95%)
  other arithmetic  2.75 us (2%)
    pallas_call x1, Pallas kernels, body(): pl.pallas_call(kernel, out_shape=(jax.ShapeDtypeStruct((PADDED, BPD * BLO...  112 us
    transpose x1, other arithmetic, body(): return (labels.T, prototypes)  2.75 us

profile of v5, /device:TPU:1, one launch (start us, length us, event | category | flops | bytes accessed | tf_op | source)
XLA Modules:
  0.0 115.9 jit_solution(15953454847543699837)
XLA Ops:
  0.6 111.8 %shard_map.59 = (bf16[1536,512]{1,0:T(8,128)(2,1)}, f32[4,128]{1,0:T(4,128)}, f32[48,1376]{1,0:T(8,128)}) custom-call(s32[5,64]{1,0:T(8,128)} %bitcast.7, s32[1,512]{1,0:T(1,128)} %bitcast.8, bf16[1376,512]{1,0:T(8,128)(2,1)} %bitcast.6, bf16[512,768]{1,0:T(8,128)(2,1)} %f_hbm.1), custom_call_target="tpu_custom_call" | custom-call | tf_op jit(solution)/shard_map/pallas_call | solution.py:466
  112.5 0.0 copy-start
  112.5 2.8 %fusion = bf16[512,1376]{0,1:T(8,128)(2,1)} fusion(f32[512]{0:T(512)} %bitcast.9, bf16[1536,512]{1,0:T(8,128)(2,1)} %get-tuple-element.5), kind=kLoop, calls=%fused_computation.1 | loop fusion | flops 2113536 | bytes 2820096 | tf_op jit(solution)/shard_map/transpose | solution.py:517
  115.2 0.0 copy-done
  115.2 0.7 copy.7
Async XLA Ops:
  112.5 2.8 %copy-start = (f32[48,1376]{1,0:T(8,128)S(1)}, f32[48,1376]{1,0:T(8,128)}, u32[]{:S(2)}) copy-start(f32[48,1376]{1,0:T(8,128)} %get-tuple-element.11) | copy-start | bytes 792580
